TPU v7x, 32 devices: a whole 2x2x4 slice. The times are simulated.
32 devices in a mesh: dp: 8 (over y, x, core), fsdp: 4 (over z).
Axes of the slice: x: 2, y: 2, z: 4, core: 2. Of those that a mesh axis runs over, the one named last changes fastest.
Arguments:
- rollout_rows: bfloat16 [4096, 8192], P(('dp', 'fsdp')), may hold values from -6 to 6
- lengths: int32 [32, 8], P(('dp', 'fsdp')), may hold values from 1 to 32, as said below
- dest: int32 [32, 8], P(('dp', 'fsdp')), may hold values from 0 to 7, as said below
- offset: int32 [32, 8], P(('dp', 'fsdp')), may hold values from 0 to 96, as said below
- query: bfloat16 [4096, 4096], P(('dp', 'fsdp')), may hold values from -100 to 100
- key_rows: bfloat16 [4096, 512], P(('dp', 'fsdp')), may hold values from -5 to 5
- value_weight: bfloat16 [8192, 512], P('fsdp'), may hold values from -0.0625 to 0.0625
- d_out: bfloat16 [4096, 4096], P(('dp', 'fsdp')), may hold values from -6 to 6
Outputs:
- attn_out: bfloat16 [4096, 4096], P(('dp', 'fsdp'))
- grad_query: bfloat16 [4096, 4096], P(('dp', 'fsdp'))
- grad_key: bfloat16 [4096, 512], P(('dp', 'fsdp'))
- grad_input: bfloat16 [4096, 8192], P(('dp', 'fsdp'))
- grad_weight: float32 [8192, 512], P(('dp', 'fsdp'))
Inputs may be any that keep to these rules, and one draw needn't show every extreme that they name: Each rollout device's 8 lengths sum to 128. `dest`: the learner has the sender's fsdp index; the sequences of one device go to 8 different learner devices. `offset`: the sequences that a learner device receives cover its 128 rows exactly once; on every learner device the last of them is one of 32 rows.
All inputs are finite; a program needn't handle non-finite values.
Results may differ from a plain program's by a relative error of at most 0.006.
Values may be sent and summed in bfloat16 or wider, within the bound.
A program may use at most 128 MiB of HBM per device.

v0:
```python
import math

import jax
import jax.numpy as jnp
from jax import lax
from jax.sharding import PartitionSpec as P

HEAD_SIZE = 128
QUERY_HEADS = 32
KEY_VALUE_HEADS = 4


def attend(block_queries, block_keys, block_values, segment, gradient_block):
    row_count_total = block_queries.shape[0]
    share_ratio = QUERY_HEADS // KEY_VALUE_HEADS
    score_scale = 1.0 / math.sqrt(HEAD_SIZE)
    heads_queries = block_queries.reshape(row_count_total, KEY_VALUE_HEADS, share_ratio, HEAD_SIZE)
    heads_keys = block_keys.reshape(row_count_total, KEY_VALUE_HEADS, HEAD_SIZE)
    heads_values = block_values.reshape(row_count_total, KEY_VALUE_HEADS, HEAD_SIZE)
    gradient_heads = gradient_block.reshape(
        row_count_total, KEY_VALUE_HEADS, share_ratio, HEAD_SIZE
    )
    logit_scores = (
        jnp.einsum("euaz,nuz->uaen", heads_queries, heads_keys, preferred_element_type=jnp.float32)
        * score_scale
    )
    position = jnp.arange(row_count_total, dtype=jnp.int32)
    allowed = (segment[:, None] == segment[None, :]) & (position[None, :] <= position[:, None])
    logit_scores = jnp.where(allowed, logit_scores, -1e30)
    highest = jnp.max(logit_scores, axis=-1, keepdims=True)
    expo = jnp.exp(logit_scores - highest)
    probs = expo / jnp.sum(expo, axis=-1, keepdims=True)
    probs_reduced = probs.astype(jnp.bfloat16)
    attention_output = jnp.einsum(
        "yxmd,dya->myxa", probs_reduced, heads_values, preferred_element_type=jnp.float32
    )
    attention_output = attention_output.reshape(row_count_total, QUERY_HEADS * HEAD_SIZE).astype(
        jnp.bfloat16
    )
    gradient_probs = jnp.einsum(
        "euaz,nuz->uaen", gradient_heads, heads_values, preferred_element_type=jnp.float32
    )
    value_gradient = jnp.einsum(
        "lbjm,jlbw->mlw", probs_reduced, gradient_heads, preferred_element_type=jnp.float32
    )
    value_gradient = value_gradient.reshape(row_count_total, KEY_VALUE_HEADS * HEAD_SIZE).astype(
        jnp.bfloat16
    )
    inner = jnp.sum(probs * gradient_probs, axis=-1, keepdims=True)
    gradient_scores = (probs * (gradient_probs - inner) * score_scale).astype(jnp.bfloat16)
    query_gradient = jnp.einsum(
        "yxmd,dya->myxa", gradient_scores, heads_keys, preferred_element_type=jnp.float32
    )
    key_gradient = jnp.einsum(
        "lbjm,jlbw->mlw", gradient_scores, heads_queries, preferred_element_type=jnp.float32
    )
    return (
        attention_output,
        query_gradient.reshape(row_count_total, QUERY_HEADS * HEAD_SIZE).astype(jnp.bfloat16),
        key_gradient.reshape(row_count_total, KEY_VALUE_HEADS * HEAD_SIZE).astype(jnp.bfloat16),
        value_gradient,
    )


def local(rollout_rows, lengths, dest, offset, query, key_rows, value_weight, d_out):
    count_dp = lax.axis_size("dp")
    count_fsdp = lax.axis_size("fsdp")
    tok_rows = rollout_rows.shape[0]
    width = rollout_rows.shape[1]
    longest = 2 * tok_rows // lengths.shape[1]
    seq_len = lengths[0]
    starts = jnp.cumsum(seq_len) - seq_len
    targets = jnp.arange(count_dp, dtype=jnp.int32)
    matched = dest[0][None, :] == targets[:, None]
    sel_start = jnp.sum(jnp.where(matched, starts[None, :], 0), axis=1)
    sel_len = jnp.sum(jnp.where(matched, seq_len[None, :], 0), axis=1)
    sel_offset = jnp.sum(jnp.where(matched, offset[0][None, :], 0), axis=1)
    slot_index = jnp.arange(longest, dtype=jnp.int32)
    source_row = jnp.clip(sel_start[:, None] + slot_index[None, :], 0, tok_rows - 1)
    in_use = slot_index[None, :] < sel_len[:, None]
    packed = jnp.take(rollout_rows, source_row.reshape(-1), axis=0).reshape(
        count_dp, longest, width
    )
    packed = jnp.where(in_use[:, :, None], packed, jnp.zeros((), jnp.bfloat16))
    header = jnp.stack([sel_offset, sel_len], axis=1)
    arrived = lax.all_to_all(packed, "dp", split_axis=0, concat_axis=0, tiled=True)
    landing = lax.all_to_all(header, "dp", split_axis=0, concat_axis=0, tiled=True)
    row_ids = jnp.arange(tok_rows, dtype=jnp.int32)
    land_off = landing[:, 0]
    land_len = landing[:, 1]
    inside = (row_ids[:, None] >= land_off[None, :]) & (
        row_ids[:, None] < land_off[None, :] + land_len[None, :]
    )
    sender = jnp.sum(jnp.where(inside, targets[None, :], 0), axis=1)
    within = jnp.sum(jnp.where(inside, row_ids[:, None] - land_off[None, :], 0), axis=1)
    learner_rows = jnp.take(
        arrived.reshape(count_dp * longest, width), sender * longest + within, axis=0
    )
    full_weight = lax.all_gather(value_weight, "fsdp", axis=0, tiled=True)
    values = jnp.dot(learner_rows, full_weight, preferred_element_type=jnp.float32).astype(
        jnp.bfloat16
    )
    attention_output, query_gradient, key_gradient, value_gradient = attend(
        query, key_rows, values, sender, d_out
    )
    grad_input = lax.dot_general(
        value_gradient, full_weight, (((1,), (1,)), ((), ())), preferred_element_type=jnp.float32
    ).astype(jnp.bfloat16)
    partial_dp = lax.psum_scatter(
        lax.dot_general(
            learner_rows,
            value_gradient,
            (((0,), (0,)), ((), ())),
            preferred_element_type=jnp.float32,
        ),
        "dp",
        scatter_dimension=0,
        tiled=True,
    )
    grad_weight = lax.psum_scatter(partial_dp, "fsdp", scatter_dimension=0, tiled=True)
    total_rows = tok_rows * count_dp * count_fsdp
    grad_weight = grad_weight * (1.0 / math.sqrt(total_rows))
    return (attention_output, query_gradient, key_gradient, grad_input, grad_weight)


def solution(mesh):
    in_specs = (
        P(("dp", "fsdp"), None),
        P(("dp", "fsdp"), None),
        P(("dp", "fsdp"), None),
        P(("dp", "fsdp"), None),
        P(("dp", "fsdp"), None),
        P(("dp", "fsdp"), None),
        P("fsdp", None),
        P(("dp", "fsdp"), None),
    )
    out_specs = (
        P(("dp", "fsdp"), None),
        P(("dp", "fsdp"), None),
        P(("dp", "fsdp"), None),
        P(("dp", "fsdp"), None),
        P(("dp", "fsdp"), None),
    )
    return jax.shard_map(local, mesh=mesh, in_specs=in_specs, out_specs=out_specs, check_vma=False)
```

profile of v0, /device:TPU:1, one launch (start us, length us, event | category | flops | bytes accessed | tf_op | source)
XLA Modules:
  0.0 301.0 jit_solution(7585224751188122253)
XLA Ops:
  8.0 0.0 copy-start
  8.0 1.0 reduce-window_clone.1
  9.0 0.7 subtract_bitcast_fusion
  9.7 0.8 select_reduce_fusion.4
  10.5 0.7 copy.45
  11.2 5.2 %all-to-all-start = ((s32[8,1,2]{2,1,0:T(1,128)}), s32[8,1,2]{2,1,0:T(1,128)S(1)}, u32[]{:S(2)}, u32[]{:S(2)}) async-start(s32[8,1,2]{2,1,0:T(1,128)} %copy.45), calls=%async_computation | async-start | bytes 8192 | tf_op jit(solution)/shard_map/all_to_all | solution.py:87
  16.4 0.1 add_clamp_fusion
  16.5 0.1 iota_compare_fusion.1
  16.5 0.1 min.12
  16.6 0.0 copy-done
  16.7 5.2 %gather_fusion = bf16[256,8192]{1,0:T(8,128)(2,1)} fusion(bf16[128,8192]{1,0:T(8,128)(2,1)S(1)} %copy-done, s32[1024]{0:T(1024)S(1)} %pad_clamp_fusion.1), kind=kCustom, calls=%fused_computation | custom fusion | bytes 8389632 | tf_op jit(solution)/shard_map/jit(_take)/gather | solution.py:81
  21.8 4.6 %select_select_fusion = bf16[8,32,8192]{2,1,0:T(8,128)(2,1)} fusion(bf16[8,32,8192]{2,1,0:T(8,128)(2,1)} %bitcast.87, pred[8,32]{1,0:T(8,128)(4,1)S(1)} %get-tuple-element.28, pred[8,32]{1,0:T(8,128)(4,1)S(1)} %get-tuple-element.27), kind=kLoop, calls=%fused_computation.5 | loop fusion | flops 4194304 | bytes 8389120 | tf_op jit(solution)/shard_map/jit(_where)/select_n | solution.py:84
  26.5 0.0 copy-start.3
  26.5 0.0 copy-start.1
  26.5 0.0 all-to-all-done
  26.5 4.7 %all-to-all-start.1 = ((bf16[8,32,8192]{2,1,0:T(8,128)(2,1)}), bf16[8,32,8192]{2,1,0:T(8,128)(2,1)}, u32[]{:S(2)}, u32[]{:S(2)}) async-start(bf16[8,32,8192]{2,1,0:T(8,128)(2,1)} %select_select_fusion), calls=%async_computation.1 | async-start | bytes 8388608 | tf_op jit(solution)/shard_map/all_to_all | solution.py:86
  31.1 0.0 reduce-scatter.3.cloned.1.call-start
  31.2 0.0 copy-done.3
  31.2 0.1 copy.67
  31.4 0.0 copy-done.1
  31.4 1.4 copy.80
  32.8 1.6 copy.81
  34.4 0.1 copy.46
  34.5 0.1 select_reduce_fusion.2
  34.6 0.1 fusion.20
  34.7 3.5 %fusion.31 = (f32[4,8,128]{2,1,0:T(8,128)S(1)}, f32[4,8,128,128]{2,3,1,0:T(8,128)}) fusion(pred[128,128]{0,1:T(8,128)(4,1)S(1)} %fusion.20, bf16[128,4,128,1]{0,2,3,1:T(8,128)(2,1)S(1)} %copy.67, bf16[128,4,8,128]{0,3,2,1:T(8,128)(2,1)} %bitcast.90), kind=kOutput, calls=%fused_computation.70 | convolution fusion | flops 136315008 | bytes 3309568 | tf_op jit(solution)/shard_map/sub | solution.py:31
  38.1 2.0 fusion.7
  40.2 36.6 %all-to-all-done.1 = bf16[8,32,8192]{2,1,0:T(8,128)(2,1)} async-done(((bf16[8,32,8192]{2,1,0:T(8,128)(2,1)}), bf16[8,32,8192]{2,1,0:T(8,128)(2,1)}, u32[]{:S(2)}, u32[]{:S(2)}) %all-to-all-start.1) | async-done | bytes 4194336 | tf_op jit(solution)/shard_map/all_to_all | solution.py:86
  76.7 7.8 %gather_fusion.1 = bf16[128,8192]{1,0:T(8,128)(2,1)} fusion(bf16[256,8192]{1,0:T(8,128)(2,1)} %bitcast.12, s32[1024]{0:T(1024)S(1)} %pad_clamp_fusion), kind=kCustom, calls=%fused_computation.1 | custom fusion | bytes 4194816 | tf_op jit(solution)/shard_map/jit(_take)/gather | solution.py:96
  84.6 9.8 %fusion.12 = f32[8192,512]{1,0:T(8,128)} fusion(bf16[128,512]{0,1:T(8,128)(2,1)S(1)} %bitcast.94, bf16[128,8192]{1,0:T(8,128)(2,1)} %gather_fusion.1, pred[128]{0:T(512)(128)(4,1)S(1)} %compare_and_fusion.1), kind=kOutput, calls=%fused_computation.27 | convolution fusion | flops 1074790400 | bytes 19005568 | tf_op jit(solution)/shard_map/dot_general | solution.py:110
  94.3 0.0 reduce-scatter.3.cloned.1.call-update
  94.3 0.0 all-gather.2.cloned.1.call-start
  94.4 0.5 all-gather.2.cloned.1.call-update
  94.9 0.2 reduce-scatter.5.cloned.1.call-start
  95.1 117.6 %reduce-scatter.3.cloned.1.call-done = f32[1024,512]{1,0:T(8,128)} async-done(((f32[8192,512]{1,0:T(8,128)}), f32[1024,512]{1,0:T(8,128)}) %reduce-scatter.3.cloned.1.call-update) | async-done | bytes 2097168 | tf_op jit(solution)/shard_map/reduce_scatter | solution.py:109
  212.7 0.0 reduce-scatter.5.cloned.1.call-update
  212.7 35.7 %all-gather.2.cloned.1.call-done = bf16[8192,512]{1,0:T(8,128)(2,1)} async-done(((bf16[2048,512]{1,0:T(8,128)(2,1)}), bf16[8192,512]{1,0:T(8,128)(2,1)}) %all-gather.2.cloned.1.call-update) | async-done | bytes 8388624 | tf_op jit(solution)/shard_map/all_gather | solution.py:99
  248.4 6.0 %convolution_convert_fusion.3 = bf16[128,512]{1,0:T(8,128)(2,1)} fusion(bf16[8192,512]{1,0:T(8,128)(2,1)} %all-gather.2.cloned.1.call-done, bf16[128,8192]{1,0:T(8,128)(2,1)} %gather_fusion.1, pred[128]{0:T(512)(128)(4,1)S(1)} %compare_and_fusion.1), kind=kOutput, calls=%fused_computation.21 | convolution fusion | flops 1074855936 | bytes 10616960 | tf_op jit(solution)/shard_map/dot_general | solution.py:100
  254.4 1.0 reshape.164
  255.4 3.1 %convolution_convert_fusion.2 = bf16[4,128,8,128]{3,1,2,0:T(8,128)(2,1)} fusion(bf16[128,4,128,1]{2,1,0,3:T(4,128)(2,1)S(1)} %bitcast.96, f32[4,8,128,128]{2,3,1,0:T(8,128)} %get-tuple-element.26, f32[4,8,128]{2,1,0:T(8,128)S(1)} %get-tuple-element.25), kind=kOutput, calls=%fused_computation.16 | convolution fusion | flops 135790592 | bytes 3293184 | tf_op jit(solution)/shard_map/yxmd,dya->myxa/dot_general | solution.py:34
  258.5 2.3 copy.59
  260.7 1.7 fusion.16
  262.5 5.5 %convolution_convert_fusion.1 = bf16[4,8,128,128]{2,3,1,0:T(8,128)(2,1)} fusion(bf16[128,4,128,1]{0,2,3,1:T(8,128)(2,1)S(1)} %copy.67, f32[4,128,128,8]{2,1,3,0:T(8,128)} %fusion.16, f32[4,8,128,128]{2,3,1,0:T(8,128)} %get-tuple-element.26, f32[4,8,128]{2,1,0:T(8,128)S(1)} %get-tuple-element.25), kind=kOutput, calls=%fused_computation.15 | convolution fusion | flops 138416256 | bytes 5390336 | tf_op jit(solution)/shard_map/yxmd,dya->myxa/dot_general | solution.py:51
  268.0 0.0 copy-start.2
  268.0 2.4 copy.60
  270.3 0.0 copy-done.2
  270.3 4.4 %fusion.6 = bf16[4,128,128]{1,2,0:T(8,128)(2,1)S(1)} fusion(bf16[128,4,8,128]{0,3,2,1:T(8,128)(2,1)S(1)} %bitcast.91, f32[4,128,128,8]{2,1,3,0:T(8,128)} %fusion.16, f32[4,8,128,128]{2,3,1,0:T(8,128)} %get-tuple-element.26, f32[4,8,128]{2,1,0:T(8,128)S(1)} %get-tuple-element.25), kind=kOutput, calls=%fused_computation.19 | convolution fusion | flops 137957504 | bytes 5390336 | tf_op jit(solution)/shard_map/lbjm,jlbw->mlw/dot_general | solution.py:54
  274.8 0.8 copy.61
  275.5 7.6 %convolution_convert_fusion = bf16[128,8192]{1,0:T(8,128)(2,1)} fusion(bf16[128,512]{0,1:T(8,128)(2,1)S(1)} %bitcast.95, bf16[8192,512]{1,0:T(8,128)(2,1)} %all-gather.2.cloned.1.call-done), kind=kOutput, calls=%fused_computation.4 | convolution fusion | flops 1074790400 | bytes 10616832 | tf_op jit(solution)/shard_map/dot_general | solution.py:106
  283.1 8.6 %reduce-scatter.5.cloned.1.call-done = f32[256,512]{1,0:T(8,128)} async-done(((f32[1024,512]{1,0:T(8,128)}), f32[256,512]{1,0:T(8,128)}) %reduce-scatter.5.cloned.1.call-update) | async-done | bytes 524304 | tf_op jit(solution)/shard_map/reduce_scatter | solution.py:120
  291.7 1.9 broadcast_multiply_fusion
  (9 shorter events, 0.1 us)
Async XLA Ops:
  8.0 8.6 %copy-start = (bf16[128,8192]{1,0:T(8,128)(2,1)S(1)}, bf16[128,8192]{1,0:T(8,128)(2,1)}, u32[]{:S(2)}) copy-start(bf16[128,8192]{1,0:T(8,128)(2,1)} %param.8) | copy-start | bytes 6291460
  11.2 15.3 %all-to-all-start = ((s32[8,1,2]{2,1,0:T(1,128)}), s32[8,1,2]{2,1,0:T(1,128)S(1)}, u32[]{:S(2)}, u32[]{:S(2)}) async-start(s32[8,1,2]{2,1,0:T(1,128)} %copy.45), calls=%async_computation | async-start | bytes 8192 | tf_op jit(solution)/shard_map/all_to_all | solution.py:87
  26.5 4.7 %copy-start.3 = (bf16[128,512]{1,0:T(8,128)(2,1)S(1)}, bf16[128,512]{1,0:T(8,128)(2,1)}, u32[]{:S(2)}) copy-start(bf16[128,512]{1,0:T(8,128)(2,1)} %param.13) | copy-start | bytes 393220
  26.5 4.9 %copy-start.1 = (bf16[128,4096]{1,0:T(8,128)(2,1)S(1)}, bf16[128,4096]{1,0:T(8,128)(2,1)}, u32[]{:S(2)}) copy-start(bf16[128,4096]{1,0:T(8,128)(2,1)} %param.12) | copy-start | bytes 3145732
  26.5 50.3 %all-to-all-start.1 = ((bf16[8,32,8192]{2,1,0:T(8,128)(2,1)}), bf16[8,32,8192]{2,1,0:T(8,128)(2,1)}, u32[]{:S(2)}, u32[]{:S(2)}) async-start(bf16[8,32,8192]{2,1,0:T(8,128)(2,1)} %select_select_fusion), calls=%async_computation.1 | async-start | bytes 8388608 | tf_op jit(solution)/shard_map/all_to_all | solution.py:86
  31.1 181.6 %reduce-scatter.3.cloned.1.call-start = ((), (), s32[]{:S(2)}) async-start(), calls=%async_computation.5 | async-start | bytes 18874368 | tf_op jit(solution)/shard_map/reduce_scatter | solution.py:109
  94.3 154.1 %all-gather.2.cloned.1.call-start = ((), (), s32[]{:S(2)}) async-start(), calls=%async_computation.4 | async-start | bytes 10485760 | tf_op jit(solution)/shard_map/all_gather | solution.py:99
  94.9 196.8 %reduce-scatter.5.cloned.1.call-start = ((), (), s32[]{:S(2)}) async-start(), calls=%async_computation.6 | async-start | bytes 2621440 | tf_op jit(solution)/shard_map/reduce_scatter | solution.py:120
  268.0 2.4 copy-start.2
Sparse Core Ops, SparseCore 0:
  94.5 118.2 reduce-scatter.2
Sparse Core Ops, SparseCore 1:
  96.4 152.0 all-gather.1
  250.6 41.1 reduce-scatter.4
where the time goes:
time: 303 us; the launch traced here: 301 us
  waiting for transfers between devices  199 us (66%)
  matrix products  43.5 us (14%)
  local copies, waits for them, and re-layouts  23.3 us (8%)
  between operations  15.6 us (5%)
  starting transfers between devices  10.2 us (3%)
  other arithmetic  9.37 us (3%)
    reduce_scatter x1, waiting for transfers between devices, local(): lax.psum_scatter(lax.dot_general(learner_rows, value_gradient, (((0,), (0...  118 us
    all_to_all x1, waiting for transfers between devices, local(): lax.all_to_all(packed, 'dp', split_axis=0, concat_axis=0, tiled=True)  36.6 us
    all_gather x1, waiting for transfers between devices, local(): full_weight = lax.all_gather(value_weight, 'fsdp', axis=0, tiled=True)  35.7 us
    dot_general x1, matrix products, local(): lax.dot_general(learner_rows, value_gradient, (((0,), (0,)), ((), ())), p...  9.76 us
    reduce_scatter x1, waiting for transfers between devices, local(): lax.psum_scatter(partial_dp, 'fsdp', scatter_dimension=0, tiled=True)  8.61 us
    gather x1, local copies, waits for them, and re-layouts, local(): jnp.take(arrived.reshape(count_dp * longest, width), sender * longest + w...  7.81 us
    dot_general x1, matrix products, local(): lax.dot_general(value_gradient, full_weight, (((1,), (1,)), ((), ())), pr...  7.57 us
  transfers between devices with their start and end apart: 5, of which 4 were waited for; matrix products, arithmetic and copies ran while one was open for 18% of the time, Pallas kernels for 0%

commit v1 on v0

--- a/solution.py
+++ b/solution.py
@@ -62,64 +62,66 @@
     )
 
 
+def tables(plan, tok_rows):
+    seq_len, dest, offset = plan[:, 0], plan[:, 1], plan[:, 2]
+    order = jnp.arange(seq_len.shape[1], dtype=jnp.int32)
+    earlier = order[None, :] < order[:, None]
+    starts = jnp.sum(jnp.where(earlier[None], seq_len[:, None, :], 0), axis=2)
+    rows = jnp.arange(tok_rows, dtype=jnp.int32)[None, :, None]
+    inside = (rows >= starts[:, None, :]) & (rows < (starts + seq_len)[:, None, :])
+    landing = (dest * tok_rows + offset - starts)[:, None, :] + rows
+    return jnp.sum(jnp.where(inside, landing, 0), axis=2).reshape(-1)
+
+
+def senders(plan, me, tok_rows):
+    seq_len, dest, offset = plan[:, 0], plan[:, 1], plan[:, 2]
+    mine = dest == me
+    land_off = jnp.sum(jnp.where(mine, offset, 0), axis=1)
+    land_len = jnp.sum(jnp.where(mine, seq_len, 0), axis=1)
+    rows = jnp.arange(tok_rows, dtype=jnp.int32)[:, None]
+    inside = (rows >= land_off[None, :]) & (rows < (land_off + land_len)[None, :])
+    source = jnp.arange(plan.shape[0], dtype=jnp.int32)
+    return jnp.sum(jnp.where(inside, source[None, :], 0), axis=1)
+
+
 def local(rollout_rows, lengths, dest, offset, query, key_rows, value_weight, d_out):
-    count_dp = lax.axis_size("dp")
-    count_fsdp = lax.axis_size("fsdp")
+    n_dp = lax.axis_size("dp")
+    n_fsdp = lax.axis_size("fsdp")
+    me = lax.axis_index("dp")
     tok_rows = rollout_rows.shape[0]
-    width = rollout_rows.shape[1]
-    longest = 2 * tok_rows // lengths.shape[1]
-    seq_len = lengths[0]
-    starts = jnp.cumsum(seq_len) - seq_len
-    targets = jnp.arange(count_dp, dtype=jnp.int32)
-    matched = dest[0][None, :] == targets[:, None]
-    sel_start = jnp.sum(jnp.where(matched, starts[None, :], 0), axis=1)
-    sel_len = jnp.sum(jnp.where(matched, seq_len[None, :], 0), axis=1)
-    sel_offset = jnp.sum(jnp.where(matched, offset[0][None, :], 0), axis=1)
-    slot_index = jnp.arange(longest, dtype=jnp.int32)
-    source_row = jnp.clip(sel_start[:, None] + slot_index[None, :], 0, tok_rows - 1)
-    in_use = slot_index[None, :] < sel_len[:, None]
-    packed = jnp.take(rollout_rows, source_row.reshape(-1), axis=0).reshape(
-        count_dp, longest, width
+    column = tok_rows * n_dp
+    plan = lax.all_gather(jnp.concatenate([lengths, dest, offset], axis=0), "dp", axis=0)
+    shared = lax.all_to_all(rollout_rows, "dp", split_axis=1, concat_axis=0, tiled=True)
+    block = value_weight.shape[0] // n_dp
+    piece = lax.dynamic_slice_in_dim(value_weight, me * block, block, axis=0)
+    pairs = [(a * n_fsdp + b, b * n_dp + a) for a in range(n_dp) for b in range(n_fsdp)]
+    piece = lax.ppermute(piece, ("dp", "fsdp"), pairs)
+    weight = lax.all_gather(piece, "fsdp", axis=0, tiled=True)
+    landing = tables(plan, tok_rows)
+    pick = (jnp.arange(column, dtype=jnp.int32)[:, None] == landing[None, :]).astype(jnp.bfloat16)
+    rows = jnp.dot(pick, shared, preferred_element_type=jnp.float32).astype(jnp.bfloat16)
+    partial = jnp.dot(rows, weight, preferred_element_type=jnp.float32).astype(jnp.bfloat16)
+    parts = lax.all_to_all(
+        partial.reshape(n_dp, tok_rows, partial.shape[1]), "dp", split_axis=0, concat_axis=0, tiled=True
     )
-    packed = jnp.where(in_use[:, :, None], packed, jnp.zeros((), jnp.bfloat16))
-    header = jnp.stack([sel_offset, sel_len], axis=1)
-    arrived = lax.all_to_all(packed, "dp", split_axis=0, concat_axis=0, tiled=True)
-    landing = lax.all_to_all(header, "dp", split_axis=0, concat_axis=0, tiled=True)
-    row_ids = jnp.arange(tok_rows, dtype=jnp.int32)
-    land_off = landing[:, 0]
-    land_len = landing[:, 1]
-    inside = (row_ids[:, None] >= land_off[None, :]) & (
-        row_ids[:, None] < land_off[None, :] + land_len[None, :]
+    values = jnp.sum(parts.astype(jnp.float32), axis=0).astype(jnp.bfloat16)
+    attention_output, query_gradient, key_gradient, value_gradient = attend(
+        query, key_rows, values, senders(plan, me, tok_rows), d_out
     )
-    sender = jnp.sum(jnp.where(inside, targets[None, :], 0), axis=1)
-    within = jnp.sum(jnp.where(inside, row_ids[:, None] - land_off[None, :], 0), axis=1)
-    learner_rows = jnp.take(
-        arrived.reshape(count_dp * longest, width), sender * longest + within, axis=0
-    )
-    full_weight = lax.all_gather(value_weight, "fsdp", axis=0, tiled=True)
-    values = jnp.dot(learner_rows, full_weight, preferred_element_type=jnp.float32).astype(
-        jnp.bfloat16
-    )
-    attention_output, query_gradient, key_gradient, value_gradient = attend(
-        query, key_rows, values, sender, d_out
-    )
-    grad_input = lax.dot_general(
-        value_gradient, full_weight, (((1,), (1,)), ((), ())), preferred_element_type=jnp.float32
-    ).astype(jnp.bfloat16)
-    partial_dp = lax.psum_scatter(
+    gathered = lax.all_gather(value_gradient, "dp", axis=0, tiled=True)
+    grad_weight = lax.psum_scatter(
         lax.dot_general(
-            learner_rows,
-            value_gradient,
-            (((0,), (0,)), ((), ())),
-            preferred_element_type=jnp.float32,
+            rows, gathered, (((0,), (0,)), ((), ())), preferred_element_type=jnp.float32
         ),
-        "dp",
+        "fsdp",
         scatter_dimension=0,
         tiled=True,
     )
-    grad_weight = lax.psum_scatter(partial_dp, "fsdp", scatter_dimension=0, tiled=True)
-    total_rows = tok_rows * count_dp * count_fsdp
-    grad_weight = grad_weight * (1.0 / math.sqrt(total_rows))
+    grad_weight = grad_weight * (1.0 / math.sqrt(column * n_fsdp))
+    share = lax.dot_general(
+        gathered, weight, (((1,), (1,)), ((), ())), preferred_element_type=jnp.float32
+    ).astype(jnp.bfloat16)
+    grad_input = lax.all_to_all(share, "dp", split_axis=0, concat_axis=1, tiled=True)
     return (attention_output, query_gradient, key_gradient, grad_input, grad_weight)
 
 

time: 303 us -> 168 us (0.55)
  the two profiles are of different devices: /device:TPU:1 before, /device:TPU:0 now
where the time goes in v1:
time: 168 us; the launch traced here: 167 us
  waiting for transfers between devices  62.9 us (37%)
  matrix products  38.7 us (23%)
  local copies, waits for them, and re-layouts  22.4 us (13%)
  starting transfers between devices  14.1 us (8%)
  between operations  13.9 us (8%)
  blocking collectives  10.3 us (6%)
  other arithmetic  4.77 us (3%)
    all_to_all x1, waiting for transfers between devices, local(): lax.all_to_all(rollout_rows, 'dp', split_axis=1, concat_axis=0, tiled=True)  30.3 us
    all_gather x1, waiting for transfers between devices, local(): weight = lax.all_gather(piece, 'fsdp', axis=0, tiled=True)  16.3 us
    all_to_all x1, waiting for transfers between devices, local(): lax.all_to_all(partial.reshape(n_dp, tok_rows, partial.shape[1]), 'dp', s...  11.2 us
    all_gather x1, blocking collectives, local(): lax.all_gather(jnp.concatenate([lengths, dest, offset], axis=0), 'dp', ax...  10.3 us
    unnamed x14, local copies, waits for them, and re-layouts  10.2 us
    dot_general x1, matrix products, attend(): jnp.einsum('yxmd,dya->myxa', gradient_scores, heads_keys, preferred_eleme...  5.38 us
    dot_general x1, matrix products, local(): jnp.dot(pick, shared, preferred_element_type=jnp.float32)  5.25 us
    all_to_all x1, waiting for transfers between devices, local(): lax.all_to_all(share, 'dp', split_axis=0, concat_axis=1, tiled=True)  5 us
  transfers between devices with their start and end apart: 7, of which 4 were waited for; matrix products, arithmetic and copies ran while one was open for 31% of the time, Pallas kernels for 0%

profile of v1, /device:TPU:0, one launch (start us, length us, event | category | flops | bytes accessed | tf_op | source)
XLA Modules:
  0.0 167.1 jit_solution(17855206566767428514)
XLA Ops:
  7.2 0.0 copy-start
  7.2 0.0 all-gather.7.cloned.1.call-start
  7.2 0.8 add_bitcast_fusion
  8.1 10.3 %all-gather.1 = s32[8,3,8]{2,1,0:T(4,128)S(1)} all-gather(s32[1,3,8]{2,1,0:T(4,128)S(1)} %add_bitcast_fusion), channel_id=2, replica_groups=mesh['dp'=8,'fsdp'=4] {'dp'}, dimensions={0}, use_global_device_ids=true | all-gather | bytes 864 | tf_op jit(solution)/shard_map/all_gather | solution.py:93
  18.4 0.1 select_reduce_fusion.3
  18.6 0.1 select_reduce_fusion.2
  18.7 0.1 fusion.19
  18.8 0.9 reshape.70
  19.7 0.1 copy.113
  19.9 2.3 %copy.127 = bf16[128,4096]{0,1:T(8,128)(2,1)} copy(bf16[128,4096]{1,0:T(8,128)(2,1)} %param.12) | data formatting | bytes 2097152 | tf_op jit(solution)/shard_map/reshape | solution.py:17
  22.2 1.6 copy.128
  23.8 3.4 %fusion.31 = (f32[4,8,128]{2,1,0:T(8,128)S(1)}, f32[4,8,128,128]{2,3,1,0:T(8,128)}) fusion(pred[128,128]{0,1:T(8,128)(4,1)S(1)} %fusion.19, bf16[128,4,128,1]{0,2,3,1:T(8,128)(2,1)S(1)} %copy.113, bf16[128,4,8,128]{0,3,2,1:T(8,128)(2,1)} %bitcast.113), kind=kOutput, calls=%fused_computation.59 | convolution fusion | flops 136315008 | bytes 3309568 | tf_op jit(solution)/shard_map/sub | solution.py:31
  27.2 0.0 copy-start.3
  27.2 2.7 %fusion.10 = bf16[4,128,128]{1,2,0:T(8,128)(2,1)} fusion(bf16[128,4,8,128]{0,3,2,1:T(8,128)(2,1)S(1)} %bitcast.108, f32[4,8,128,128]{2,3,1,0:T(8,128)} %get-tuple-element.38, f32[4,8,128]{2,1,0:T(8,128)S(1)} %get-tuple-element.37), kind=kOutput, calls=%fused_computation.21 | convolution fusion | flops 135331840 | bytes 3293184 | tf_op jit(solution)/shard_map/lbjm,jlbw->mlw/dot_general | solution.py:43
  29.9 0.0 copy-done.3
  29.9 0.0 all-gather.7.cloned.1.call-update
  30.0 4.1 %copy.90 = bf16[128,8192]{0,1:T(8,128)(2,1)} copy(bf16[128,8192]{1,0:T(8,128)(2,1)} %param.8) | data formatting | bytes 4194304 | tf_op args[0]
  34.0 4.4 %all-to-all-start = ((bf16[128,8,1024]{0,2,1:T(8,128)(2,1)}), bf16[128,8,1024]{0,2,1:T(8,128)(2,1)}, u32[]{:S(2)}, u32[]{:S(2)}) async-start(bf16[128,8,1024]{0,2,1:T(8,128)(2,1)} %bitcast.107), calls=%async_computation | async-start | bytes 4194304 | tf_op jit(solution)/shard_map/all_to_all | solution.py:94
  38.4 0.0 all-gather.5.cloned.1.call-start
  38.5 0.0 copy-done
  38.5 0.7 collective-permute-start
  39.2 0.0 collective-permute-done
  39.2 0.0 copy-start.2
  39.2 0.7 copy-done.2
  39.9 0.0 all-gather.5.cloned.1.call-update
  39.9 0.0 reduce-scatter.2.cloned.1.call-start
  40.0 0.2 select_reduce_fusion.1
  40.2 0.1 select_reduce_fusion
  40.3 30.3 %all-to-all-done = bf16[128,8,1024]{0,2,1:T(8,128)(2,1)} async-done(((bf16[128,8,1024]{0,2,1:T(8,128)(2,1)}), bf16[128,8,1024]{0,2,1:T(8,128)(2,1)}, u32[]{:S(2)}, u32[]{:S(2)}) %all-to-all-start) | async-done | bytes 2097184 | tf_op jit(solution)/shard_map/all_to_all | solution.py:94
  70.7 3.9 %copy.91 = bf16[8,128,1024]{2,1,0:T(8,128)(2,1)} copy(bf16[8,128,1024]{1,2,0:T(8,128)(2,1)} %bitcast.7) | data formatting | bytes 4194304 | tf_op jit(solution)/shard_map/all_to_all | solution.py:94
  74.6 5.3 %fusion.7 = bf16[1024,1024]{1,0:T(8,128)(2,1)} fusion(bf16[1024,1024]{1,0:T(8,128)(2,1)} %bitcast.112, s32[1024]{0:T(1024)S(1)} %bitcast.130), kind=kOutput, calls=%fused_computation.12 | convolution fusion | flops 2149580800 | bytes 4198400 | tf_op jit(solution)/shard_map/dot_general | solution.py:102
  79.8 0.0 all-gather.7.cloned.1.call-done
  79.8 4.5 %fusion.33 = f32[1024,512]{1,0:T(8,128)} fusion(bf16[1024,1024]{1,0:T(8,128)(2,1)} %fusion.7, bf16[1024,512]{0,1:T(8,128)(2,1)} %all-gather.7.cloned.1.call-done), kind=kOutput, calls=%fused_computation.61 | convolution fusion | flops 1073741824 | bytes 5242880 | tf_op jit(solution)/shard_map/dot_general | solution.py:113
  84.4 0.0 reduce-scatter.2.cloned.1.call-update
  84.4 16.3 %all-gather.5.cloned.1.call-done = bf16[1024,512]{1,0:T(8,128)(2,1)} async-done(((bf16[256,512]{1,0:T(8,128)(2,1)}), bf16[1024,512]{1,0:T(8,128)(2,1)}) %all-gather.5.cloned.1.call-update) | async-done | bytes 1048592 | tf_op jit(solution)/shard_map/all_gather | solution.py:99
  100.7 4.1 %convolution_convert_fusion.3 = bf16[1024,512]{1,0:T(8,128)(2,1)} fusion(bf16[1024,1024]{1,0:T(8,128)(2,1)} %fusion.7, bf16[1024,512]{1,0:T(8,128)(2,1)} %all-gather.5.cloned.1.call-done), kind=kOutput, calls=%fused_computation.17 | convolution fusion | flops 1074266112 | bytes 4194304 | tf_op jit(solution)/shard_map/dot_general | solution.py:103
  104.7 4.2 %all-to-all-start.1 = ((bf16[8,128,512]{2,1,0:T(8,128)(2,1)}), bf16[8,128,512]{2,1,0:T(8,128)(2,1)}, u32[]{:S(2)}, u32[]{:S(2)}) async-start(bf16[8,128,512]{2,1,0:T(8,128)(2,1)} %bitcast.115), calls=%async_computation.1 | async-start | bytes 2097152 | tf_op jit(solution)/shard_map/all_to_all | solution.py:104
  109.0 4.2 %convolution_convert_fusion = bf16[1024,1024]{1,0:T(8,128)(2,1)} fusion(bf16[1024,512]{0,1:T(8,128)(2,1)} %all-gather.7.cloned.1.call-done, bf16[1024,512]{1,0:T(8,128)(2,1)} %all-gather.5.cloned.1.call-done), kind=kOutput, calls=%fused_computation.13 | convolution fusion | flops 1074790400 | bytes 4194304 | tf_op jit(solution)/shard_map/dot_general | solution.py:121
  113.2 11.2 %all-to-all-done.1 = bf16[8,128,512]{2,1,0:T(8,128)(2,1)} async-done(((bf16[8,128,512]{2,1,0:T(8,128)(2,1)}), bf16[8,128,512]{2,1,0:T(8,128)(2,1)}, u32[]{:S(2)}, u32[]{:S(2)}) %all-to-all-start.1) | async-done | bytes 1048608 | tf_op jit(solution)/shard_map/all_to_all | solution.py:104
  124.4 0.0 copy-start.4
  124.4 4.7 %all-to-all-start.2 = ((bf16[8,128,1024]{2,1,0:T(8,128)(2,1)}), bf16[8,128,1024]{2,1,0:T(8,128)(2,1)}, u32[]{:S(2)}, u32[]{:S(2)}) async-start(bf16[8,128,1024]{2,1,0:T(8,128)(2,1)} %bitcast.110), calls=%async_computation.2 | async-start | bytes 4194304 | tf_op jit(solution)/shard_map/all_to_all | solution.py:124
  129.1 1.4 reduce_sum.80
  130.5 0.1 copy.92
  130.6 0.0 copy-done.4
  130.6 3.0 %convolution_convert_fusion.2 = bf16[4,128,8,128]{3,1,2,0:T(8,128)(2,1)} fusion(bf16[128,4,128,1]{0,2,3,1:T(8,128)(2,1)S(1)} %bitcast.118, f32[4,8,128,128]{2,3,1,0:T(8,128)} %get-tuple-element.38, f32[4,8,128]{2,1,0:T(8,128)S(1)} %copy-done.4), kind=kOutput, calls=%fused_computation.16 | convolution fusion | flops 135790592 | bytes 3293184 | tf_op jit(solution)/shard_map/yxmd,dya->myxa/dot_general | solution.py:34
  133.6 2.3 %copy.105 = bf16[128,4096]{1,0:T(8,128)(2,1)} copy(bf16[128,4096]{0,1:T(8,128)(2,1)} %bitcast.117) | data formatting | bytes 2097152
  135.9 1.8 %fusion.32 = f32[4,128,128,8]{2,1,3,0:T(8,128)} fusion(bf16[128,4,128,1]{0,2,3,1:T(8,128)(2,1)S(1)} %bitcast.119, bf16[128,4,8,128]{0,3,2,1:T(8,128)(2,1)S(1)} %bitcast.109), kind=kOutput, calls=%fused_computation.60 | convolution fusion | flops 134217728 | bytes 3276800 | tf_op jit(solution)/shard_map/euaz,nuz->uaen/dot_general | solution.py:40
  137.7 5.4 %convolution_convert_fusion.1 = bf16[4,8,128,128]{2,3,1,0:T(8,128)(2,1)} fusion(bf16[128,4,128,1]{0,2,3,1:T(8,128)(2,1)S(1)} %copy.113, f32[4,128,128,8]{2,1,3,0:T(8,128)} %fusion.32, f32[4,8,128,128]{2,3,1,0:T(8,128)} %get-tuple-element.38, f32[4,8,128]{2,1,0:T(8,128)S(1)} %copy-done.4), kind=kOutput, calls=%fused_computation.15 | convolution fusion | flops 138416256 | bytes 5390336 | tf_op jit(solution)/shard_map/yxmd,dya->myxa/dot_general | solution.py:51
  143.1 0.0 copy-start.1
  143.1 2.4 %copy.106 = bf16[128,4096]{1,0:T(8,128)(2,1)} copy(bf16[128,4096]{0,1:T(8,128)(2,1)} %bitcast.116) | data formatting | bytes 2097152
  145.4 0.0 copy-done.1
  145.4 4.4 %fusion.9 = bf16[4,128,128]{1,2,0:T(8,128)(2,1)S(1)} fusion(bf16[128,4,8,128]{0,3,2,1:T(8,128)(2,1)S(1)} %bitcast.114, f32[4,128,128,8]{2,1,3,0:T(8,128)} %fusion.32, f32[4,8,128,128]{2,3,1,0:T(8,128)} %get-tuple-element.38, f32[4,8,128]{2,1,0:T(8,128)S(1)} %copy-done.4), kind=kOutput, calls=%fused_computation.20 | convolution fusion | flops 137957504 | bytes 5390336 | tf_op jit(solution)/shard_map/lbjm,jlbw->mlw/dot_general | solution.py:54
  149.8 0.8 copy.107
  150.6 5.0 %all-to-all-done.2 = bf16[8,128,1024]{2,1,0:T(8,128)(2,1)} async-done(((bf16[8,128,1024]{2,1,0:T(8,128)(2,1)}), bf16[8,128,1024]{2,1,0:T(8,128)(2,1)}, u32[]{:S(2)}, u32[]{:S(2)}) %all-to-all-start.2) | async-done | bytes 2097184 | tf_op jit(solution)/shard_map/all_to_all | solution.py:124
  155.6 3.1 %copy.129 = bf16[8,16,8,1024]{3,2,0,1:T(8,128)(2,1)} copy(bf16[8,16,8,1024]{3,2,1,0:T(8,128)(2,1)} %bitcast.49) | data formatting | bytes 4194304 | tf_op jit(solution)/shard_map/all_to_all | solution.py:124
  158.7 0.0 reduce-scatter.2.cloned.1.call-done
  158.7 1.9 %broadcast_multiply_fusion = f32[256,512]{1,0:T(8,128)} fusion(f32[256,512]{1,0:T(8,128)} %reduce-scatter.2.cloned.1.call-done), kind=kLoop, calls=%fused_computation.29 | loop fusion | flops 131072 | bytes 1048576 | tf_op jit(solution)/shard_map/mul | solution.py:120
  (5 shorter events, 0.1 us)
Async XLA Ops:
  7.2 31.3 %copy-start = (bf16[2048,512]{1,0:T(8,128)(2,1)S(1)}, bf16[2048,512]{1,0:T(8,128)(2,1)}, u32[]{:S(2)}) copy-start(bf16[2048,512]{1,0:T(8,128)(2,1)} %param.14) | copy-start | bytes 6291460
  7.2 72.7 %all-gather.7.cloned.1.call-start = ((), (), s32[]{:S(2)}) async-start(), calls=%async_computation.5 | async-start | bytes 1179648 | tf_op jit(solution)/shard_map/all_gather | solution.py:111
  27.2 2.7 %copy-start.3 = (f32[4,8,128]{2,1,0:T(8,128)}, f32[4,8,128]{2,1,0:T(8,128)S(1)}, u32[]{:S(2)}) copy-start(f32[4,8,128]{2,1,0:T(8,128)S(1)} %get-tuple-element.37) | copy-start | bytes 49156
  34.0 36.6 %all-to-all-start = ((bf16[128,8,1024]{0,2,1:T(8,128)(2,1)}), bf16[128,8,1024]{0,2,1:T(8,128)(2,1)}, u32[]{:S(2)}, u32[]{:S(2)}) async-start(bf16[128,8,1024]{0,2,1:T(8,128)(2,1)} %bitcast.107), calls=%async_computation | async-start | bytes 4194304 | tf_op jit(solution)/shard_map/all_to_all | solution.py:94
  38.4 62.2 %all-gather.5.cloned.1.call-start = ((), (), s32[]{:S(2)}) async-start(), calls=%async_computation.4 | async-start | bytes 1310720 | tf_op jit(solution)/shard_map/all_gather | solution.py:99
  38.5 0.7 collective-permute-start
  39.2 0.7 copy-start.2
  39.9 118.8 %reduce-scatter.2.cloned.1.call-start = ((), (), s32[]{:S(2)}) async-start(), calls=%async_computation.6 | async-start | bytes 2621440 | tf_op jit(solution)/shard_map/reduce_scatter | solution.py:112
  104.7 19.7 %all-to-all-start.1 = ((bf16[8,128,512]{2,1,0:T(8,128)(2,1)}), bf16[8,128,512]{2,1,0:T(8,128)(2,1)}, u32[]{:S(2)}, u32[]{:S(2)}) async-start(bf16[8,128,512]{2,1,0:T(8,128)(2,1)} %bitcast.115), calls=%async_computation.1 | async-start | bytes 2097152 | tf_op jit(solution)/shard_map/all_to_all | solution.py:104
  124.4 6.2 %copy-start.4 = (f32[4,8,128]{2,1,0:T(8,128)S(1)}, f32[4,8,128]{2,1,0:T(8,128)}, u32[]{:S(2)}) copy-start(f32[4,8,128]{2,1,0:T(8,128)} %copy-done.3) | copy-start | bytes 49156
  124.4 31.2 %all-to-all-start.2 = ((bf16[8,128,1024]{2,1,0:T(8,128)(2,1)}), bf16[8,128,1024]{2,1,0:T(8,128)(2,1)}, u32[]{:S(2)}, u32[]{:S(2)}) async-start(bf16[8,128,1024]{2,1,0:T(8,128)(2,1)} %bitcast.110), calls=%async_computation.2 | async-start | bytes 4194304 | tf_op jit(solution)/shard_map/all_to_all | solution.py:124
  143.1 2.4 %copy-start.1 = (bf16[128,4096]{0,1:T(8,128)(2,1)S(1)}, bf16[128,4096]{0,1:T(8,128)(2,1)}, u32[]{:S(2)}) copy-start(bf16[128,4096]{0,1:T(8,128)(2,1)} %copy.127) | copy-start | bytes 3145732
Sparse Core Ops, SparseCore 0:
  30.1 37.2 all-gather.6
  69.5 31.0 all-gather.4
  103.0 43.3 reduce-scatter.1

commit v2 on v1

v2 whole, which is shorter than its diff:
```python
import functools
import math

import jax
import jax.numpy as jnp
from jax import lax
from jax.experimental import pallas as pl
from jax.experimental.pallas import tpu as pltpu
from jax.sharding import PartitionSpec as P

HEAD_SIZE = 128
QUERY_HEADS = 32
KEY_VALUE_HEADS = 4
MESH = pl.DeviceIdType.MESH
F32 = jnp.float32
BF16 = jnp.bfloat16


def dot(a, b, contract):
    return lax.dot_general(a, b, ((contract[:1], contract[1:]), ((), ())), preferred_element_type=F32)


def kernel(
    n_dp, n_fsdp, scale,
    x_ref, landing_ref, q_ref, k_ref, w_ref, d_ref,
    out_ref, gq_ref, gk_ref, gi_ref, gw_ref,
    shared, land, weight, pick, part, part_out, parts, values, probs, gathered, share, gwp, gwr,
    x_send, x_recv, l_send, l_recv, p_send, p_recv, g_send, g_recv, i_send, i_recv,
    w_send, w_recv, s_send, s_recv, perm_send, perm_recv, local_sem,
):
    a = lax.axis_index("dp")
    b = lax.axis_index("fsdp")
    tok = x_ref.shape[0]
    cols = shared.shape[2]
    block = cols // n_fsdp
    group = QUERY_HEADS // KEY_VALUE_HEADS
    given = b * n_dp + a
    to_a, to_b = given // n_fsdp, given % n_fsdp
    taken = a * n_fsdp + b
    from_a, from_b = taken % n_dp, taken // n_dp
    away = given != taken

    def dp_peer(i):
        return lax.rem(a + i, n_dp)

    def fsdp_peer(i):
        return lax.rem(b + i, n_fsdp)

    def over_dp(body):
        lax.fori_loop(1, n_dp, lambda i, c: (body(dp_peer(i)), c)[1], 0)

    def over_fsdp(body):
        lax.fori_loop(1, n_fsdp, lambda i, c: (body(fsdp_peer(i)), c)[1], 0)

    barrier = pltpu.get_barrier_semaphore()
    over_dp(lambda p: pl.semaphore_signal(barrier, inc=1, device_id={"dp": p}, device_id_type=MESH))
    over_fsdp(lambda p: pl.semaphore_signal(barrier, inc=1, device_id={"fsdp": p}, device_id_type=MESH))

    @pl.when(away)
    def _():
        pl.semaphore_signal(
            barrier, inc=1, device_id={"dp": from_a, "fsdp": from_b}, device_id_type=MESH
        )
        pl.semaphore_wait(barrier, n_dp + n_fsdp - 1)

    @pl.when(jnp.logical_not(away))
    def _():
        pl.semaphore_wait(barrier, n_dp + n_fsdp - 2)

    def remote(src, dst, send, recv, **where):
        return pltpu.make_async_remote_copy(
            src_ref=src, dst_ref=dst, send_sem=send, recv_sem=recv, device_id=where, device_id_type=MESH
        )

    def columns(p):
        return pl.ds(pl.multiple_of(p * cols, cols), cols)

    def x_copy(p, slot):
        return remote(x_ref.at[:, columns(p)], shared.at[slot], x_send.at[p], x_recv.at[slot], dp=p)

    def l_copy(p, slot):
        return remote(landing_ref, land.at[slot], l_send.at[p], l_recv.at[slot], dp=p)

    def p_copy(p, slot):
        return remote(part_out.at[p], parts.at[slot], p_send.at[p], p_recv.at[slot], dp=p)

    def g_copy(p, slot):
        return remote(gathered.at[a], gathered.at[slot], g_send.at[p], g_recv.at[slot], dp=p)

    def i_copy(p, slot):
        return remote(share.at[p], gi_ref.at[:, columns(slot)], i_send.at[p], i_recv.at[slot], dp=p)

    def w_copy(p, slot):
        return remote(weight.at[b], weight.at[slot], w_send.at[p], w_recv.at[slot], fsdp=p)

    def s_copy(p, slot):
        return remote(gwp.at[p], gwr.at[slot], s_send.at[p], s_recv.at[slot], fsdp=p)

    piece = w_ref.at[pl.ds(pl.multiple_of(a * block, block), block), :]
    perm = remote(piece, weight.at[to_b], perm_send, perm_recv, dp=to_a, fsdp=to_b)
    perm_in = remote(piece, weight.at[b], perm_send, perm_recv, dp=to_a, fsdp=to_b)
    perm_own = pltpu.make_async_copy(piece, weight.at[b], local_sem.at[1])

    @pl.when(away)
    def _():
        perm.start()

    @pl.when(jnp.logical_not(away))
    def _():
        perm_own.start()

    over_dp(lambda p: l_copy(p, a).start())
    over_dp(lambda p: x_copy(p, a).start())
    own = pltpu.make_async_copy(x_ref.at[:, columns(a)], shared.at[a], local_sem.at[0])
    own.start()
    land[a] = landing_ref[...]

    over_dp(lambda p: l_copy(p, p).wait_recv())
    line = lax.broadcasted_iota(jnp.int32, (n_dp * tok, tok), 0)
    for p in range(n_dp):
        hit = line == land[p][0:1, :]
        pick[:, p * tok : (p + 1) * tok] = jnp.where(hit, 1.0, 0.0).astype(BF16)

    @pl.when(away)
    def _():
        perm_in.wait_recv()

    @pl.when(jnp.logical_not(away))
    def _():
        perm_own.wait()

    over_fsdp(lambda p: w_copy(p, b).start())

    mine = pick[pl.ds(pl.multiple_of(a * tok, tok), tok), :]
    source = lax.broadcasted_iota(jnp.int32, (n_dp * tok, 128), 0) // tok
    lane = lax.broadcasted_iota(jnp.int32, (n_dp * tok, 128), 1)
    sender = dot(mine, jnp.where(source == lane, 1.0, 0.0).astype(BF16), (1, 0)).astype(BF16)
    same = dot(sender, sender, (1, 1)) > 0.5
    t_id = lax.broadcasted_iota(jnp.int32, (tok, tok), 0)
    s_id = lax.broadcasted_iota(jnp.int32, (tok, tok), 1)
    bias = jnp.where(same & (s_id <= t_id), 0.0, -1e30)
    root = 1.0 / math.sqrt(HEAD_SIZE)

    def head(g, i):
        return pl.ds(pl.multiple_of((g * group + i) * HEAD_SIZE, HEAD_SIZE), HEAD_SIZE)

    def stacked(ref, g):
        return jnp.concatenate([ref[:, head(g, i)] for i in range(group)], axis=0)

    def kv(g):
        return pl.ds(pl.multiple_of(g * HEAD_SIZE, HEAD_SIZE), HEAD_SIZE)

    def forward(g, c):
        logits = dot(stacked(q_ref, g), k_ref[:, kv(g)], (1, 1)) * root
        logits = logits.reshape(group, tok, tok)
        logits = jnp.where(bias[None] < 0.0, -1e30, logits)
        expo = jnp.exp(logits - jnp.max(logits, axis=-1, keepdims=True))
        probs[g] = (expo / jnp.sum(expo, axis=-1, keepdims=True)).reshape(group * tok, tok)
        return c

    lax.fori_loop(0, KEY_VALUE_HEADS, forward, 0)

    over_fsdp(lambda p: w_copy(p, p).wait_recv())
    full = weight[...].reshape(cols, weight.shape[2])
    own.wait()
    part[a] = dot(shared[a], full, (1, 0)).astype(BF16)

    def project(p):
        x_copy(p, p).wait_recv()
        part[p] = dot(shared[p], full, (1, 0)).astype(BF16)

    over_dp(project)
    every = part[...].reshape(n_dp * tok, part.shape[2])

    def order(p):
        return dot(pick[pl.ds(pl.multiple_of(p * tok, tok), tok), :], every, (1, 0)).astype(BF16)

    def deal(p):
        part_out[p] = order(p)
        p_copy(p, a).start()

    over_dp(deal)
    parts[a] = order(a)
    over_dp(lambda p: p_copy(p, p).wait_recv())
    total = parts[0].astype(F32)
    for p in range(1, n_dp):
        total += parts[p].astype(F32)
    values[...] = total.astype(BF16)

    def backward(g, c):
        v = values[:, kv(g)]
        d = stacked(d_ref, g)
        pr = probs[g]
        pb = pr.astype(BF16)
        att = dot(pb, v, (1, 0)).astype(BF16)
        gathered[a, :, kv(g)] = dot(pb, d, (0, 0)).astype(BF16)
        dp = dot(d, v, (1, 1))
        inner = jnp.sum(pr * dp, axis=-1, keepdims=True)
        ds = (pr * (dp - inner) * root).astype(BF16)
        gq = dot(ds, k_ref[:, kv(g)], (1, 0)).astype(BF16)
        gk_ref[:, kv(g)] = dot(ds, stacked(q_ref, g), (0, 0)).astype(BF16)
        for i in range(group):
            out_ref[:, head(g, i)] = att[i * tok : (i + 1) * tok]
            gq_ref[:, head(g, i)] = gq[i * tok : (i + 1) * tok]
        return c

    lax.fori_loop(0, KEY_VALUE_HEADS, backward, 0)

    over_dp(lambda p: g_copy(p, a).start())
    share[a] = dot(gathered[a], full, (1, 1)).astype(BF16)
    keep = pltpu.make_async_copy(share.at[a], gi_ref.at[:, columns(a)], local_sem.at[2])
    keep.start()

    def spread(p):
        g_copy(p, p).wait_recv()
        share[p] = dot(gathered[p], full, (1, 1)).astype(BF16)
        i_copy(p, a).start()

    over_dp(spread)
    learned = gathered[...].reshape(n_dp * tok, gathered.shape[2])
    back = dot(pick[...], learned, (0, 0)).astype(BF16)
    tokens = shared[...].reshape(n_dp * tok, cols)
    gwp[...] = dot(tokens, back, (0, 0)).reshape(n_fsdp, block, back.shape[1])
    over_fsdp(lambda p: s_copy(p, b).start())
    gwr[b] = gwp[b]
    over_fsdp(lambda p: s_copy(p, p).wait_recv())
    grad = gwr[0]
    for p in range(1, n_fsdp):
        grad += gwr[p]
    gw_ref[...] = grad * scale

    over_dp(lambda p: i_copy(p, p).wait_recv())
    keep.wait()

    def drain(p):
        x_copy(p, a).wait_send()
        l_copy(p, a).wait_send()
        p_copy(p, a).wait_send()
        g_copy(p, a).wait_send()
        i_copy(p, a).wait_send()

    over_dp(drain)

    def drain_fsdp(p):
        w_copy(p, b).wait_send()
        s_copy(p, b).wait_send()

    over_fsdp(drain_fsdp)

    @pl.when(away)
    def _():
        perm.wait_send()


def local(rollout_rows, lengths, dest, offset, query, key_rows, value_weight, d_out):
    n_dp = lax.axis_size("dp")
    n_fsdp = lax.axis_size("fsdp")
    tok, width = rollout_rows.shape
    kvw = value_weight.shape[1]
    cols = width // n_dp
    block = cols // n_fsdp
    seq = lengths.shape[1]
    order = jnp.arange(seq, dtype=jnp.int32)
    starts = jnp.sum(jnp.where(order[None, :] < order[:, None], lengths, 0), axis=1)[:, None]
    rows = jnp.arange(tok, dtype=jnp.int32)[None, :]
    inside = (rows >= starts) & (rows < starts + lengths[0][:, None])
    place = (dest[0] * tok + offset[0])[:, None] - starts + rows
    landing = jnp.sum(jnp.where(inside, place, 0), axis=0)
    landing = jnp.broadcast_to(landing[None, :], (8, tok))
    vmem = pl.BlockSpec(memory_space=pltpu.VMEM)
    hbm = pl.BlockSpec(memory_space=pl.ANY)
    dma = pltpu.SemaphoreType.DMA
    shape = jax.ShapeDtypeStruct
    group = QUERY_HEADS // KEY_VALUE_HEADS
    return pl.pallas_call(
        functools.partial(kernel, n_dp, n_fsdp, 1.0 / math.sqrt(tok * n_dp * n_fsdp)),
        out_shape=(
            shape(query.shape, BF16),
            shape(query.shape, BF16),
            shape(key_rows.shape, BF16),
            shape(rollout_rows.shape, BF16),
            shape((block, kvw), F32),
        ),
        in_specs=[hbm, vmem, vmem, vmem, hbm, vmem],
        out_specs=(vmem, vmem, vmem, hbm, vmem),
        scratch_shapes=[
            pltpu.VMEM((n_dp, tok, cols), BF16),
            pltpu.VMEM((n_dp, 8, tok), jnp.int32),
            pltpu.VMEM((n_fsdp, block, kvw), BF16),
            pltpu.VMEM((n_dp * tok, n_dp * tok), BF16),
            pltpu.VMEM((n_dp, tok, kvw), BF16),
            pltpu.VMEM((n_dp, tok, kvw), BF16),
            pltpu.VMEM((n_dp, tok, kvw), BF16),
            pltpu.VMEM((tok, kvw), BF16),
            pltpu.VMEM((KEY_VALUE_HEADS, group * tok, tok), F32),
            pltpu.VMEM((n_dp, tok, kvw), BF16),
            pltpu.VMEM((n_dp, tok, cols), BF16),
            pltpu.VMEM((n_fsdp, block, kvw), F32),
            pltpu.VMEM((n_fsdp, block, kvw), F32),
        ]
        + [dma((n_dp,))] * 10
        + [dma((n_fsdp,))] * 4
        + [dma, dma, dma((3,))],
        compiler_params=pltpu.CompilerParams(
            collective_id=0, has_side_effects=True, vmem_limit_bytes=56 * 1024 * 1024
        ),
    )(rollout_rows, landing, query, key_rows, value_weight, d_out)


def solution(mesh):
    rows = P(("dp", "fsdp"), None)
    return jax.shard_map(
        local,
        mesh=mesh,
        in_specs=(rows, rows, rows, rows, rows, rows, P("fsdp", None), rows),
        out_specs=(rows,) * 5,
        check_vma=False,
    )
```

time: 168 us -> 137 us (0.82)
  the two profiles are of different devices: /device:TPU:0 before, /device:TPU:9 now
where the time goes in v2:
time: 137 us
  Pallas kernels  128 us (93%)
  local copies, waits for them, and re-layouts  6.86 us (5%)
  other arithmetic  1.55 us (1%)
    pallas_call x1, Pallas kernels, local(): pl.pallas_call(functools.partial(kernel, n_dp, n_fsdp, 1.0 / math.sqrt(to...  128 us
    unnamed x13, local copies, waits for them, and re-layouts  6.26 us

profile of v2, /device:TPU:9, one launch (start us, length us, event | category | flops | bytes accessed | tf_op | source)
XLA Modules:
  0.0 137.2 jit_solution(9940385387788314640)
XLA Ops:
  0.6 0.8 select_reduce_fusion.1
  1.4 0.7 bitcast_add_fusion
  2.1 0.1 select_reduce_fusion
  2.2 0.6 broadcast_in_dim.33.landing_ref
  2.8 128.1 %shard_map.119 = (bf16[128,4096]{1,0:T(8,128)(2,1)}, bf16[128,4096]{1,0:T(8,128)(2,1)}, bf16[128,512]{1,0:T(8,128)(2,1)}, bf16[128,8192]{1,0:T(8,128)(2,1)}, f32[256,512]{1,0:T(8,128)}) custom-call(bf16[128,8192]{1,0:T(8,128)(2,1)} %x_ref.1, s32[8,128]{1,0:T(8,128)} %broadcast_in_dim.33.landing_ref, bf16[128,4096]{1,0:T(8,128)(2,1)} %q_ref.1, ...), custom_call_target="tpu_custom_call" | custom-call | tf_op jit(solution)/shard_map/pallas_call | solution.py:275
  130.9 0.0 copy-start.1
  130.9 0.0 copy-start.3
  130.9 0.0 copy-start
  130.9 2.4 %copy.18 = bf16[128,4096]{1,0:T(8,128)(2,1)} copy(bf16[128,4096]{1,0:T(8,128)(2,1)} %get-tuple-element.12) | data formatting | bytes 2097152
  133.3 0.0 copy-done.1
  133.3 1.0 copy.19
  134.3 0.0 copy-done.3
  134.3 0.7 copy.20
  135.0 0.0 copy-done
  135.0 0.0 copy-start.2
  135.0 1.3 copy.21
  136.3 0.1 copy-done.2
  136.4 0.8 copy.22
Async XLA Ops:
  130.9 2.5 %copy-start.1 = (bf16[128,4096]{1,0:T(8,128)(2,1)S(1)}, bf16[128,4096]{1,0:T(8,128)(2,1)}, u32[]{:S(2)}) copy-start(bf16[128,4096]{1,0:T(8,128)(2,1)} %get-tuple-element.13) | copy-start | bytes 3145732
  130.9 3.4 %copy-start.3 = (bf16[128,512]{1,0:T(8,128)(2,1)S(1)}, bf16[128,512]{1,0:T(8,128)(2,1)}, u32[]{:S(2)}) copy-start(bf16[128,512]{1,0:T(8,128)(2,1)} %get-tuple-element.14) | copy-start | bytes 393220
  130.9 4.1 %copy-start = (bf16[128,8192]{1,0:T(8,128)(2,1)S(1)}, bf16[128,8192]{1,0:T(8,128)(2,1)}, u32[]{:S(2)}) copy-start(bf16[128,8192]{1,0:T(8,128)(2,1)} %get-tuple-element.15) | copy-start | bytes 6291460
  135.0 1.4 %copy-start.2 = (f32[256,512]{1,0:T(8,128)S(1)}, f32[256,512]{1,0:T(8,128)}, u32[]{:S(2)}) copy-start(f32[256,512]{1,0:T(8,128)} %get-tuple-element.16) | copy-start | bytes 1572868

commit v3 on v2

--- a/solution.py
+++ b/solution.py
@@ -24,7 +24,7 @@
     n_dp, n_fsdp, scale,
     x_ref, landing_ref, q_ref, k_ref, w_ref, d_ref,
     out_ref, gq_ref, gk_ref, gi_ref, gw_ref,
-    shared, land, weight, pick, part, part_out, parts, values, probs, gathered, share, gwp, gwr,
+    shared, land, weight, pick, part, part_out, parts, values, probs, gathered, share, gwp, gws, gwr,
     x_send, x_recv, l_send, l_recv, p_send, p_recv, g_send, g_recv, i_send, i_recv,
     w_send, w_recv, s_send, s_recv, perm_send, perm_recv, local_sem,
 ):
@@ -90,11 +90,13 @@
     def i_copy(p, slot):
         return remote(share.at[p], gi_ref.at[:, columns(slot)], i_send.at[p], i_recv.at[slot], dp=p)
 
-    def w_copy(p, slot):
-        return remote(weight.at[b], weight.at[slot], w_send.at[p], w_recv.at[slot], fsdp=p)
+    def w_copy(p, slot, sem):
+        return remote(weight.at[slot], weight.at[slot], w_send.at[sem], w_recv.at[slot], fsdp=p)
+
+    has_left, has_right = b > 0, b < n_fsdp - 1
 
     def s_copy(p, slot):
-        return remote(gwp.at[p], gwr.at[slot], s_send.at[p], s_recv.at[slot], fsdp=p)
+        return remote(gws.at[p], gwr.at[slot], s_send.at[p], s_recv.at[slot], fsdp=p)
 
     piece = w_ref.at[pl.ds(pl.multiple_of(a * block, block), block), :]
     perm = remote(piece, weight.at[to_b], perm_send, perm_recv, dp=to_a, fsdp=to_b)
@@ -120,16 +122,6 @@
     for p in range(n_dp):
         hit = line == land[p][0:1, :]
         pick[:, p * tok : (p + 1) * tok] = jnp.where(hit, 1.0, 0.0).astype(BF16)
-
-    @pl.when(away)
-    def _():
-        perm_in.wait_recv()
-
-    @pl.when(jnp.logical_not(away))
-    def _():
-        perm_own.wait()
-
-    over_fsdp(lambda p: w_copy(p, b).start())
 
     mine = pick[pl.ds(pl.multiple_of(a * tok, tok), tok), :]
     source = lax.broadcasted_iota(jnp.int32, (n_dp * tok, 128), 0) // tok
@@ -160,7 +152,40 @@
 
     lax.fori_loop(0, KEY_VALUE_HEADS, forward, 0)
 
-    over_fsdp(lambda p: w_copy(p, p).wait_recv())
+    @pl.when(away)
+    def _():
+        perm_in.wait_recv()
+
+    @pl.when(jnp.logical_not(away))
+    def _():
+        perm_own.wait()
+
+    @pl.when(has_right)
+    def _():
+        w_copy(b + 1, b, b).start()
+
+    @pl.when(has_left)
+    def _():
+        w_copy(b - 1, b, n_fsdp).start()
+
+    for step in range(1, n_fsdp):
+
+        @pl.when(b >= step)
+        def _():
+            w_copy(b - 1, b - step, b - step).wait_recv()
+
+            @pl.when(has_right)
+            def _():
+                w_copy(b + 1, b - step, b - step).start()
+
+        @pl.when(b + step < n_fsdp)
+        def _():
+            w_copy(b + 1, b + step, b + step).wait_recv()
+
+            @pl.when(has_left)
+            def _():
+                w_copy(b - 1, b + step, b + step).start()
+
     full = weight[...].reshape(cols, weight.shape[2])
     own.wait()
     part[a] = dot(shared[a], full, (1, 0)).astype(BF16)
@@ -221,12 +246,13 @@
     back = dot(pick[...], learned, (0, 0)).astype(BF16)
     tokens = shared[...].reshape(n_dp * tok, cols)
     gwp[...] = dot(tokens, back, (0, 0)).reshape(n_fsdp, block, back.shape[1])
+    gws[...] = gwp[...].astype(BF16)
     over_fsdp(lambda p: s_copy(p, b).start())
-    gwr[b] = gwp[b]
+    gwr[b] = jnp.zeros_like(gwr[b])
     over_fsdp(lambda p: s_copy(p, p).wait_recv())
-    grad = gwr[0]
-    for p in range(1, n_fsdp):
-        grad += gwr[p]
+    grad = gwp[b]
+    for p in range(n_fsdp):
+        grad += gwr[p].astype(F32)
     gw_ref[...] = grad * scale
 
     over_dp(lambda p: i_copy(p, p).wait_recv())
@@ -242,10 +268,27 @@
     over_dp(drain)
 
     def drain_fsdp(p):
-        w_copy(p, b).wait_send()
         s_copy(p, b).wait_send()
 
     over_fsdp(drain_fsdp)
+
+    @pl.when(has_right)
+    def _():
+        w_copy(b + 1, b, b).wait_send()
+
+    @pl.when(has_left)
+    def _():
+        w_copy(b - 1, b, n_fsdp).wait_send()
+
+    for step in range(1, n_fsdp):
+
+        @pl.when((b >= step) & has_right)
+        def _():
+            w_copy(b + 1, b - step, b - step).wait_send()
+
+        @pl.when((b + step < n_fsdp) & has_left)
+        def _():
+            w_copy(b - 1, b + step, b + step).wait_send()
 
     @pl.when(away)
     def _():
@@ -296,10 +339,12 @@
             pltpu.VMEM((n_dp, tok, kvw), BF16),
             pltpu.VMEM((n_dp, tok, cols), BF16),
             pltpu.VMEM((n_fsdp, block, kvw), F32),
-            pltpu.VMEM((n_fsdp, block, kvw), F32),
+            pltpu.VMEM((n_fsdp, block, kvw), BF16),
+            pltpu.VMEM((n_fsdp, block, kvw), BF16),
         ]
         + [dma((n_dp,))] * 10
-        + [dma((n_fsdp,))] * 4
+        + [dma((n_fsdp + 1,))]
+        + [dma((n_fsdp,))] * 3
         + [dma, dma, dma((3,))],
         compiler_params=pltpu.CompilerParams(
             collective_id=0, has_side_effects=True, vmem_limit_bytes=56 * 1024 * 1024

time: 137 us -> 117 us (0.85)
  the two profiles are of different devices: /device:TPU:9 before, /device:TPU:1 now
where the time goes in v3:
time: 117 us
  Pallas kernels  108 us (92%)
  local copies, waits for them, and re-layouts  6.86 us (6%)
  other arithmetic  1.55 us (1%)
    pallas_call x1, Pallas kernels, local(): pl.pallas_call(functools.partial(kernel, n_dp, n_fsdp, 1.0 / math.sqrt(to...  108 us
    unnamed x13, local copies, waits for them, and re-layouts  6.26 us

profile of v3, /device:TPU:1, one launch (start us, length us, event | category | flops | bytes accessed | tf_op | source)
XLA Modules:
  0.0 116.7 jit_solution(1365197346666419596)
XLA Ops:
  0.6 0.8 select_reduce_fusion.1
  1.4 0.7 bitcast_add_fusion
  2.1 0.1 select_reduce_fusion
  2.2 0.6 broadcast_in_dim.33.landing_ref
  2.8 107.6 %shard_map.119 = (bf16[128,4096]{1,0:T(8,128)(2,1)}, bf16[128,4096]{1,0:T(8,128)(2,1)}, bf16[128,512]{1,0:T(8,128)(2,1)}, bf16[128,8192]{1,0:T(8,128)(2,1)}, f32[256,512]{1,0:T(8,128)}) custom-call(bf16[128,8192]{1,0:T(8,128)(2,1)} %x_ref.1, s32[8,128]{1,0:T(8,128)} %broadcast_in_dim.33.landing_ref, bf16[128,4096]{1,0:T(8,128)(2,1)} %q_ref.1, ...), custom_call_target="tpu_custom_call" | custom-call | tf_op jit(solution)/shard_map/pallas_call | solution.py:318
  110.4 0.0 copy-start.1
  110.4 0.0 copy-start.3
  110.4 0.0 copy-start
  110.4 2.4 %copy.18 = bf16[128,4096]{1,0:T(8,128)(2,1)} copy(bf16[128,4096]{1,0:T(8,128)(2,1)} %get-tuple-element.12) | data formatting | bytes 2097152
  112.9 0.0 copy-done.1
  112.9 1.0 copy.19
  113.8 0.0 copy-done.3
  113.8 0.7 copy.20
  114.5 0.0 copy-done
  114.5 0.0 copy-start.2
  114.5 1.3 %copy.21 = bf16[128,8192]{1,0:T(8,128)(2,1)} copy(bf16[128,8192]{1,0:T(8,128)(2,1)S(1)} %copy-done) | data formatting | bytes 4194304
  115.8 0.1 copy-done.2
  115.9 0.8 copy.22
Async XLA Ops:
  110.4 2.5 %copy-start.1 = (bf16[128,4096]{1,0:T(8,128)(2,1)S(1)}, bf16[128,4096]{1,0:T(8,128)(2,1)}, u32[]{:S(2)}) copy-start(bf16[128,4096]{1,0:T(8,128)(2,1)} %get-tuple-element.13) | copy-start | bytes 3145732
  110.4 3.4 %copy-start.3 = (bf16[128,512]{1,0:T(8,128)(2,1)S(1)}, bf16[128,512]{1,0:T(8,128)(2,1)}, u32[]{:S(2)}) copy-start(bf16[128,512]{1,0:T(8,128)(2,1)} %get-tuple-element.14) | copy-start | bytes 393220
  110.4 4.1 %copy-start = (bf16[128,8192]{1,0:T(8,128)(2,1)S(1)}, bf16[128,8192]{1,0:T(8,128)(2,1)}, u32[]{:S(2)}) copy-start(bf16[128,8192]{1,0:T(8,128)(2,1)} %get-tuple-element.15) | copy-start | bytes 6291460
  114.5 1.4 %copy-start.2 = (f32[256,512]{1,0:T(8,128)S(1)}, f32[256,512]{1,0:T(8,128)}, u32[]{:S(2)}) copy-start(f32[256,512]{1,0:T(8,128)} %get-tuple-element.16) | copy-start | bytes 1572868

commit v4 on v2

--- a/solution.py
+++ b/solution.py
@@ -9,6 +9,7 @@
 from jax.sharding import PartitionSpec as P
 
 HEAD_SIZE = 128
+PIECES = 2
 QUERY_HEADS = 32
 KEY_VALUE_HEADS = 4
 MESH = pl.DeviceIdType.MESH
@@ -24,9 +25,9 @@
     n_dp, n_fsdp, scale,
     x_ref, landing_ref, q_ref, k_ref, w_ref, d_ref,
     out_ref, gq_ref, gk_ref, gi_ref, gw_ref,
-    shared, land, weight, pick, part, part_out, parts, values, probs, gathered, share, gwp, gwr,
+    shared, land, weight, pick, part, part_out, parts, values, probs, gathered, share, gwp, gws, gwr,
     x_send, x_recv, l_send, l_recv, p_send, p_recv, g_send, g_recv, i_send, i_recv,
-    w_send, w_recv, s_send, s_recv, perm_send, perm_recv, local_sem,
+    w_send, w_recv, s_send, s_recv, perm_send, perm_recv, perm_local, local_sem,
 ):
     a = lax.axis_index("dp")
     b = lax.axis_index("fsdp")
@@ -90,24 +91,38 @@
     def i_copy(p, slot):
         return remote(share.at[p], gi_ref.at[:, columns(slot)], i_send.at[p], i_recv.at[slot], dp=p)
 
-    def w_copy(p, slot):
-        return remote(weight.at[b], weight.at[slot], w_send.at[p], w_recv.at[slot], fsdp=p)
+    def w_copy(p, slot, sem, c):
+        rows = weight.at[slot, pl.ds(c * part_rows, part_rows)]
+        return remote(rows, rows, w_send.at[c, sem], w_recv.at[c, slot], fsdp=p)
+
+    has_left, has_right = b > 0, b < n_fsdp - 1
 
     def s_copy(p, slot):
-        return remote(gwp.at[p], gwr.at[slot], s_send.at[p], s_recv.at[slot], fsdp=p)
-
-    piece = w_ref.at[pl.ds(pl.multiple_of(a * block, block), block), :]
-    perm = remote(piece, weight.at[to_b], perm_send, perm_recv, dp=to_a, fsdp=to_b)
-    perm_in = remote(piece, weight.at[b], perm_send, perm_recv, dp=to_a, fsdp=to_b)
-    perm_own = pltpu.make_async_copy(piece, weight.at[b], local_sem.at[1])
+        return remote(gws.at[p], gwr.at[slot], s_send.at[p], s_recv.at[slot], fsdp=p)
+
+    part_rows = block // PIECES
+
+    def piece(c):
+        return w_ref.at[pl.ds(pl.multiple_of(a * block + c * part_rows, part_rows), part_rows), :]
+
+    def perm(c, slot):
+        rows = weight.at[slot, pl.ds(c * part_rows, part_rows)]
+        return remote(piece(c), rows, perm_send.at[c], perm_recv.at[c], dp=to_a, fsdp=to_b)
+
+    def perm_own(c):
+        return pltpu.make_async_copy(
+            piece(c), weight.at[b, pl.ds(c * part_rows, part_rows)], perm_local.at[c]
+        )
 
     @pl.when(away)
     def _():
-        perm.start()
+        for c in range(PIECES):
+            perm(c, to_b).start()
 
     @pl.when(jnp.logical_not(away))
     def _():
-        perm_own.start()
+        for c in range(PIECES):
+            perm_own(c).start()
 
     over_dp(lambda p: l_copy(p, a).start())
     over_dp(lambda p: x_copy(p, a).start())
@@ -120,16 +135,6 @@
     for p in range(n_dp):
         hit = line == land[p][0:1, :]
         pick[:, p * tok : (p + 1) * tok] = jnp.where(hit, 1.0, 0.0).astype(BF16)
-
-    @pl.when(away)
-    def _():
-        perm_in.wait_recv()
-
-    @pl.when(jnp.logical_not(away))
-    def _():
-        perm_own.wait()
-
-    over_fsdp(lambda p: w_copy(p, b).start())
 
     mine = pick[pl.ds(pl.multiple_of(a * tok, tok), tok), :]
     source = lax.broadcasted_iota(jnp.int32, (n_dp * tok, 128), 0) // tok
@@ -160,7 +165,43 @@
 
     lax.fori_loop(0, KEY_VALUE_HEADS, forward, 0)
 
-    over_fsdp(lambda p: w_copy(p, p).wait_recv())
+    for c in range(PIECES):
+
+        @pl.when(away)
+        def _(c=c):
+            perm(c, b).wait_recv()
+
+        @pl.when(jnp.logical_not(away))
+        def _(c=c):
+            perm_own(c).wait()
+
+        @pl.when(has_right)
+        def _(c=c):
+            w_copy(b + 1, b, b, c).start()
+
+        @pl.when(has_left)
+        def _(c=c):
+            w_copy(b - 1, b, n_fsdp, c).start()
+
+    for step in range(1, n_fsdp):
+        for c in range(PIECES):
+
+            @pl.when(b >= step)
+            def _(c=c, step=step):
+                w_copy(b - 1, b - step, b - step, c).wait_recv()
+
+                @pl.when(has_right)
+                def _():
+                    w_copy(b + 1, b - step, b - step, c).start()
+
+            @pl.when(b + step < n_fsdp)
+            def _(c=c, step=step):
+                w_copy(b + 1, b + step, b + step, c).wait_recv()
+
+                @pl.when(has_left)
+                def _():
+                    w_copy(b - 1, b + step, b + step, c).start()
+
     full = weight[...].reshape(cols, weight.shape[2])
     own.wait()
     part[a] = dot(shared[a], full, (1, 0)).astype(BF16)
@@ -221,12 +262,13 @@
     back = dot(pick[...], learned, (0, 0)).astype(BF16)
     tokens = shared[...].reshape(n_dp * tok, cols)
     gwp[...] = dot(tokens, back, (0, 0)).reshape(n_fsdp, block, back.shape[1])
+    gws[...] = gwp[...].astype(BF16)
     over_fsdp(lambda p: s_copy(p, b).start())
-    gwr[b] = gwp[b]
+    gwr[b] = jnp.zeros_like(gwr[b])
     over_fsdp(lambda p: s_copy(p, p).wait_recv())
-    grad = gwr[0]
-    for p in range(1, n_fsdp):
-        grad += gwr[p]
+    grad = gwp[b]
+    for p in range(n_fsdp):
+        grad += gwr[p].astype(F32)
     gw_ref[...] = grad * scale
 
     over_dp(lambda p: i_copy(p, p).wait_recv())
@@ -242,14 +284,33 @@
     over_dp(drain)
 
     def drain_fsdp(p):
-        w_copy(p, b).wait_send()
         s_copy(p, b).wait_send()
 
     over_fsdp(drain_fsdp)
 
-    @pl.when(away)
-    def _():
-        perm.wait_send()
+    for c in range(PIECES):
+
+        @pl.when(away)
+        def _(c=c):
+            perm(c, to_b).wait_send()
+
+        @pl.when(has_right)
+        def _(c=c):
+            w_copy(b + 1, b, b, c).wait_send()
+
+        @pl.when(has_left)
+        def _(c=c):
+            w_copy(b - 1, b, n_fsdp, c).wait_send()
+
+        for step in range(1, n_fsdp):
+
+            @pl.when((b >= step) & has_right)
+            def _(c=c, step=step):
+                w_copy(b + 1, b - step, b - step, c).wait_send()
+
+            @pl.when((b + step < n_fsdp) & has_left)
+            def _(c=c, step=step):
+                w_copy(b - 1, b + step, b + step, c).wait_send()
 
 
 def local(rollout_rows, lengths, dest, offset, query, key_rows, value_weight, d_out):
@@ -296,11 +357,14 @@
             pltpu.VMEM((n_dp, tok, kvw), BF16),
             pltpu.VMEM((n_dp, tok, cols), BF16),
             pltpu.VMEM((n_fsdp, block, kvw), F32),
-            pltpu.VMEM((n_fsdp, block, kvw), F32),
+            pltpu.VMEM((n_fsdp, block, kvw), BF16),
+            pltpu.VMEM((n_fsdp, block, kvw), BF16),
         ]
         + [dma((n_dp,))] * 10
-        + [dma((n_fsdp,))] * 4
-        + [dma, dma, dma((3,))],
+        + [dma((PIECES, n_fsdp + 1)), dma((PIECES, n_fsdp))]
+        + [dma((n_fsdp,))] * 2
+        + [dma((PIECES,))] * 3
+        + [dma((3,))],
         compiler_params=pltpu.CompilerParams(
             collective_id=0, has_side_effects=True, vmem_limit_bytes=56 * 1024 * 1024
         ),

time: 137 us -> 114 us (0.83)
  the two profiles are of different devices: /device:TPU:9 before, /device:TPU:1 now
where the time goes in v4:
time: 114 us
  Pallas kernels  105 us (92%)
  local copies, waits for them, and re-layouts  6.86 us (6%)
  other arithmetic  1.55 us (1%)
    pallas_call x1, Pallas kernels, local(): pl.pallas_call(functools.partial(kernel, n_dp, n_fsdp, 1.0 / math.sqrt(to...  105 us
    unnamed x13, local copies, waits for them, and re-layouts  6.26 us

profile of v4, /device:TPU:1, one launch (start us, length us, event | category | flops | bytes accessed | tf_op | source)
XLA Modules:
  0.0 114.0 jit_solution(15199404289948726595)
XLA Ops:
  0.6 0.8 select_reduce_fusion.1
  1.4 0.7 bitcast_add_fusion
  2.1 0.1 select_reduce_fusion
  2.2 0.6 broadcast_in_dim.33.landing_ref
  2.8 104.9 %shard_map.119 = (bf16[128,4096]{1,0:T(8,128)(2,1)}, bf16[128,4096]{1,0:T(8,128)(2,1)}, bf16[128,512]{1,0:T(8,128)(2,1)}, bf16[128,8192]{1,0:T(8,128)(2,1)}, f32[256,512]{1,0:T(8,128)}) custom-call(bf16[128,8192]{1,0:T(8,128)(2,1)} %x_ref.1, s32[8,128]{1,0:T(8,128)} %broadcast_in_dim.33.landing_ref, bf16[128,4096]{1,0:T(8,128)(2,1)} %q_ref.1, ...), custom_call_target="tpu_custom_call" | custom-call | tf_op jit(solution)/shard_map/pallas_call | solution.py:336
  107.7 0.0 copy-start.1
  107.7 0.0 copy-start.3
  107.7 0.0 copy-start
  107.8 2.4 %copy.18 = bf16[128,4096]{1,0:T(8,128)(2,1)} copy(bf16[128,4096]{1,0:T(8,128)(2,1)} %get-tuple-element.12) | data formatting | bytes 2097152
  110.2 0.0 copy-done.1
  110.2 1.0 copy.19
  111.2 0.0 copy-done.3
  111.2 0.7 copy.20
  111.8 0.0 copy-done
  111.8 0.0 copy-start.2
  111.8 1.3 %copy.21 = bf16[128,8192]{1,0:T(8,128)(2,1)} copy(bf16[128,8192]{1,0:T(8,128)(2,1)S(1)} %copy-done) | data formatting | bytes 4194304
  113.2 0.1 copy-done.2
  113.2 0.8 copy.22
Async XLA Ops:
  107.7 2.5 %copy-start.1 = (bf16[128,4096]{1,0:T(8,128)(2,1)S(1)}, bf16[128,4096]{1,0:T(8,128)(2,1)}, u32[]{:S(2)}) copy-start(bf16[128,4096]{1,0:T(8,128)(2,1)} %get-tuple-element.13) | copy-start | bytes 3145732
  107.7 3.4 %copy-start.3 = (bf16[128,512]{1,0:T(8,128)(2,1)S(1)}, bf16[128,512]{1,0:T(8,128)(2,1)}, u32[]{:S(2)}) copy-start(bf16[128,512]{1,0:T(8,128)(2,1)} %get-tuple-element.14) | copy-start | bytes 393220
  107.7 4.1 %copy-start = (bf16[128,8192]{1,0:T(8,128)(2,1)S(1)}, bf16[128,8192]{1,0:T(8,128)(2,1)}, u32[]{:S(2)}) copy-start(bf16[128,8192]{1,0:T(8,128)(2,1)} %get-tuple-element.15) | copy-start | bytes 6291460
  111.8 1.4 %copy-start.2 = (f32[256,512]{1,0:T(8,128)S(1)}, f32[256,512]{1,0:T(8,128)}, u32[]{:S(2)}) copy-start(f32[256,512]{1,0:T(8,128)} %get-tuple-element.16) | copy-start | bytes 1572868
